TPU v7x, 32 devices: a whole 2x2x4 slice. The times are simulated.
32 devices in a mesh: col: 8 (over z, x), sub: 4 (over y, core).
Axes of the slice: x: 2, y: 2, z: 4, core: 2. Of those that a mesh axis runs over, the one named last changes fastest.
Arguments:
- right_sides: float32 [16, 16384], P(None, ('col', 'sub')), may hold values from -40 to 40
- left_bases: bfloat16 [16384, 2048], P(('col', 'sub')), may hold values from -0.25 to 0.25
- right_bases: bfloat16 [32, 64, 16384], P(None, None, ('col', 'sub')), may hold values from -0.25 to 0.25
- tile_scales: float32 [32, 32, 64], P(None, ('col', 'sub')), may hold values from 0.002 to 0.03
- tile_ranks: int32 [32, 32], P(None, ('col', 'sub')), may hold values from 8 to 64, as said below
- near_field: bfloat16 [16384, 512], P(('col', 'sub')), may hold values from -0.078125 to 0.078125
- diagonal: float32 [16384], P(('col', 'sub')), may hold values from 1 to 3
Outputs:
- solution: float32 [16, 16384], P(None, ('col', 'sub'))
- residual: float32 [16, 16384], P(None, ('col', 'sub'))
Inputs may be any that keep to these rules, and one draw needn't show every extreme that they name: Tile (i, j) uses the first tile_ranks[i, j] columns of its bases; every diagonal tile uses all 64.
All inputs are finite; a program needn't handle non-finite values.
Results may differ from a plain program's by a relative error of at most 0.006.
Values may be sent and summed in bfloat16 or wider, within the bound.
A program may use at most 128 MiB of HBM per device.

v0:
```python
import jax
import jax.numpy as jnp
from jax import lax
from jax.sharding import PartitionSpec as P

ITERS = 2


highest = lax.Precision.HIGHEST


def gram_of(first_rows, second_rows):
    return jnp.dot(first_rows, second_rows.T, precision=highest)


def on_device(right_sides, left_bases, right_bases, tile_scales, tile_ranks, near_field, diagonal):
    rhs_count, cell_count = right_sides.shape
    tile_len = near_field.shape[1]
    local_tiles = cell_count // tile_len
    total_tiles = right_bases.shape[0]
    rank_len = right_bases.shape[1]
    feature_len = rhs_count * rank_len
    keep_mask = lax.broadcasted_iota(jnp.int32, tile_scales.shape, 2) < tile_ranks[:, :, None]
    weights = jnp.where(keep_mask, tile_scales, jnp.zeros_like(tile_scales))
    right_tiles = right_bases.reshape(total_tiles, rank_len, local_tiles, tile_len)
    left_tiles = left_bases.reshape(local_tiles, tile_len, total_tiles, rank_len)
    near_tiles = near_field.reshape(local_tiles, tile_len, tile_len)

    def apply_matrix(vectors):
        rounded = vectors.astype(jnp.bfloat16).reshape(rhs_count, local_tiles, tile_len)
        coefficients = jnp.einsum(
            "irkt,nkt->iknr", right_tiles, rounded, preferred_element_type=jnp.float32
        )
        coefficients = (coefficients * weights[:, :, None, :]).astype(jnp.bfloat16)
        shaped = coefficients.reshape(total_tiles, local_tiles, feature_len)
        received = lax.all_to_all(shaped, ("col", "sub"), split_axis=0, concat_axis=1, tiled=True)
        near_term = jnp.einsum(
            "kpq,nkq->nkp", near_tiles, rounded, preferred_element_type=jnp.float32
        )
        received = received.reshape(local_tiles, total_tiles, rhs_count, rank_len)
        far_term = jnp.einsum(
            "ktjr,kjnr->nkt", left_tiles, received, preferred_element_type=jnp.float32
        )
        return (
            diagonal[None, :] * vectors
            + near_term.reshape(rhs_count, cell_count)
            + far_term.reshape(rhs_count, cell_count)
        )

    start_gram = lax.psum(gram_of(right_sides, right_sides), ("col", "sub"))
    start_factor = jnp.linalg.cholesky(start_gram)
    basis_list = [jax.scipy.linalg.solve_triangular(start_factor, right_sides, lower=True)]
    hess_rows = []
    for iteration in range(ITERS):
        next_vectors = apply_matrix(basis_list[iteration])
        stacked = jnp.concatenate(basis_list, axis=0)
        projections, raw_gram = lax.psum(
            (gram_of(next_vectors, stacked), gram_of(next_vectors, next_vectors)), ("col", "sub")
        )
        next_vectors = next_vectors - jnp.dot(projections, stacked, precision=highest)
        new_gram = raw_gram - jnp.dot(projections, projections.T, precision=highest)
        factor_low = jnp.linalg.cholesky(new_gram)
        if iteration + 1 < ITERS:
            basis_list.append(
                jax.scipy.linalg.solve_triangular(factor_low, next_vectors, lower=True)
            )
        padding = jnp.zeros((rhs_count, rhs_count * (ITERS - iteration - 1)), jnp.float32)
        hess_rows.append(jnp.concatenate([projections, factor_low, padding], axis=1))
    hessenberg = jnp.concatenate(hess_rows, axis=0)
    normal_matrix = jnp.dot(hessenberg, hessenberg.T, precision=highest)
    right_term = jnp.dot(start_factor, hessenberg[:, :rhs_count].T, precision=highest)
    normal_factor = jnp.linalg.cholesky(normal_matrix)
    coordinates = jax.scipy.linalg.cho_solve((normal_factor, True), right_term.T).T
    solution = jnp.dot(coordinates, jnp.concatenate(basis_list, axis=0), precision=highest)
    residual = right_sides - apply_matrix(solution)
    return (solution, residual)


def solution(mesh):
    in_specs = (
        P(None, ("col", "sub")),
        P(("col", "sub"), None),
        P(None, None, ("col", "sub")),
        P(None, ("col", "sub"), None),
        P(None, ("col", "sub")),
        P(("col", "sub"), None),
        P(("col", "sub")),
    )
    out_specs = (P(None, ("col", "sub")), P(None, ("col", "sub")))
    return jax.shard_map(
        on_device, mesh=mesh, in_specs=in_specs, out_specs=out_specs, check_vma=False
    )
```

profile of v0, /device:TPU:0, one launch (start us, length us, event | category | flops | bytes accessed | tf_op | source)
XLA Modules:
  0.0 194.4 jit_solution(8500557873810185790)
XLA Ops:
  0.6 1.1 fusion.48
  1.7 42.1 %psum.35 = f32[16,16]{0,1:T(8,128)S(1)} all-reduce(f32[16,16]{0,1:T(8,128)S(1)} %fusion.48), channel_id=1, replica_groups=mesh['col'=8,'sub'=4] {'col','sub'}, use_global_device_ids=true, to_apply=%region_0.1 | all-reduce | flops 256 | bytes 2048 | tf_op jit(solution)/shard_map/psum | solution.py:50
  43.9 1.5 cholesky.94
  46.6 1.2 custom-call.17
  47.9 1.0 fusion.30
  53.0 4.4 %all-to-all-start = ((bf16[32,2,512]{2,1,0:T(2,128)(2,1)}), bf16[32,2,512]{2,1,0:T(2,128)(2,1)S(1)}, u32[]{:S(2)}, u32[]{:S(2)}) async-start(bf16[32,2,512]{2,1,0:T(2,128)(2,1)} %reshape.172), calls=%async_computation | async-start | bytes 131072 | tf_op jit(solution)/shard_map/all_to_all | solution.py:36
  57.4 4.0 %copy.47 = bf16[512,2048]{0,1:T(8,128)(2,1)} copy(bf16[512,2048]{1,0:T(8,128)(2,1)} %param.11) | data formatting | bytes 4194304 | tf_op args[1]
  61.6 3.1 %all-to-all-done = bf16[32,2,512]{2,1,0:T(2,128)(2,1)S(1)} async-done(((bf16[32,2,512]{2,1,0:T(2,128)(2,1)}), bf16[32,2,512]{2,1,0:T(2,128)(2,1)S(1)}, u32[]{:S(2)}, u32[]{:S(2)}) %all-to-all-start) | async-done | bytes 65568 | tf_op jit(solution)/shard_map/all_to_all | solution.py:36
  65.4 2.0 %fusion.11 = f32[16,512]{1,0:T(8,128)S(1)} fusion(f32[16,512]{1,0:T(8,128)S(1)} %convolution_add_fusion.2, bf16[32,16,64]{2,1,0:T(8,128)(2,1)S(1)} %reshape.154, bf16[512,32,64]{0,2,1:T(8,128)(2,1)} %bitcast.135), kind=kOutput, calls=%fused_computation.18 | convolution fusion | flops 33562624 | bytes 2228224 | tf_op jit(solution)/shard_map/ktjr,kjnr->nkt/dot_general | solution.py:41
  67.7 38.5 %all-reduce.1 = (f32[16,16]{1,0:T(8,128)S(1)}, f32[16,16]{0,1:T(8,128)S(1)}) all-reduce(f32[16,16]{1,0:T(8,128)S(1)} %fusion.49, f32[16,16]{0,1:T(8,128)S(1)} %fusion.50), channel_id=1, replica_groups=mesh['col'=8,'sub'=4] {'col','sub'}, use_global_device_ids=true, to_apply=%region_3.6 | all-reduce | flops 512 | bytes 4096 | tf_op jit(solution)/shard_map/psum | solution.py:57
  106.5 1.5 cholesky.105
  109.3 1.2 custom-call.18
  111.9 1.0 reduce.14
  113.5 3.7 %all-to-all-start.1 = ((bf16[32,2,512]{2,1,0:T(2,128)(2,1)}), bf16[32,2,512]{2,1,0:T(2,128)(2,1)S(1)}, u32[]{:S(2)}, u32[]{:S(2)}) async-start(bf16[32,2,512]{2,1,0:T(2,128)(2,1)} %reshape.174), calls=%async_computation.1 | async-start | bytes 131072 | tf_op jit(solution)/shard_map/all_to_all | solution.py:36
  117.5 7.2 %all-to-all-done.1 = bf16[32,2,512]{2,1,0:T(2,128)(2,1)S(1)} async-done(((bf16[32,2,512]{2,1,0:T(2,128)(2,1)}), bf16[32,2,512]{2,1,0:T(2,128)(2,1)S(1)}, u32[]{:S(2)}, u32[]{:S(2)}) %all-to-all-start.1) | async-done | bytes 65568 | tf_op jit(solution)/shard_map/all_to_all | solution.py:36
  125.2 2.0 %fusion.10 = f32[16,512]{1,0:T(8,128)S(1)} fusion(f32[16,512]{1,0:T(8,128)S(1)} %convolution_add_fusion.1, bf16[32,16,64]{2,1,0:T(8,128)(2,1)S(1)} %reshape.157, bf16[512,32,64]{0,2,1:T(8,128)(2,1)} %bitcast.136), kind=kOutput, calls=%fused_computation.15 | convolution fusion | flops 33562624 | bytes 2228224 | tf_op jit(solution)/shard_map/ktjr,kjnr->nkt/dot_general | solution.py:41
  127.5 38.5 %all-reduce = (f32[16,16]{0,1:T(8,128)S(1)}, f32[16,32]{1,0:T(8,128)S(1)}) all-reduce(f32[16,16]{0,1:T(8,128)S(1)} %fusion.51, f32[16,32]{1,0:T(8,128)S(1)} %fusion.14), channel_id=1, replica_groups=mesh['col'=8,'sub'=4] {'col','sub'}, use_global_device_ids=true, to_apply=%region_6.9 | all-reduce | flops 768 | bytes 6144 | tf_op jit(solution)/shard_map/psum | solution.py:57
  166.2 1.5 cholesky.116
  170.1 2.9 %cholesky.41 = f32[32,32]{1,0:T(8,128)S(1)} custom-call(f32[32,32]{1,0:T(8,128)S(1)} %fusion.23), custom_call_target="Cholesky" | custom-call | tf_op jit(solution)/shard_map/jit(cholesky)/cholesky | solution.py:72
  174.4 2.4 %custom-call.15 = f32[1,32,32]{1,2,0:T(8,128)S(1)} custom-call(f32[1,32,32]{2,1,0:T(8,128)S(1)} %fusion.15), custom_call_target="InvertDiagBlocksLowerTriangular" | custom-call | tf_op jit(solution)/shard_map/jit(_cho_solve)/triangular_solve | solution.py:73
  178.4 1.0 reduce.15
  180.0 3.7 %all-to-all-start.2 = ((bf16[32,2,512]{2,1,0:T(2,128)(2,1)}), bf16[32,2,512]{2,1,0:T(2,128)(2,1)S(1)}, u32[]{:S(2)}, u32[]{:S(2)}) async-start(bf16[32,2,512]{2,1,0:T(2,128)(2,1)} %reshape.176), calls=%async_computation.2 | async-start | bytes 131072 | tf_op jit(solution)/shard_map/all_to_all | solution.py:36
  184.0 7.2 %all-to-all-done.2 = bf16[32,2,512]{2,1,0:T(2,128)(2,1)S(1)} async-done(((bf16[32,2,512]{2,1,0:T(2,128)(2,1)}), bf16[32,2,512]{2,1,0:T(2,128)(2,1)S(1)}, u32[]{:S(2)}, u32[]{:S(2)}) %all-to-all-start.2) | async-done | bytes 65568 | tf_op jit(solution)/shard_map/all_to_all | solution.py:36
  191.7 2.6 %fusion.12 = f32[16,512]{1,0:T(8,128)} fusion(f32[16,512]{1,0:T(8,128)S(1)} %copy-done.2, f32[16,512]{1,0:T(8,128)S(1)} %convolution_add_fusion, bf16[32,16,64]{2,1,0:T(8,128)(2,1)S(1)} %reshape.159, bf16[512,32,64]{0,2,1:T(8,128)(2,1)} %bitcast.137), kind=kOutput, calls=%fused_computation.19 | convolution fusion | flops 33570816 | bytes 2260992 | tf_op jit(solution)/shard_map/ktjr,kjnr->nkt/dot_general | solution.py:41
  (69 shorter events, 18.3 us)
Async XLA Ops:
  0.6 49.1 %copy-start = (bf16[32,64,512]{2,1,0:T(8,128)(2,1)S(1)}, bf16[32,64,512]{2,1,0:T(8,128)(2,1)}, u32[]{:S(2)}) copy-start(bf16[32,64,512]{2,1,0:T(8,128)(2,1)} %param.12) | copy-start | bytes 6291460
  53.0 11.8 %all-to-all-start = ((bf16[32,2,512]{2,1,0:T(2,128)(2,1)}), bf16[32,2,512]{2,1,0:T(2,128)(2,1)S(1)}, u32[]{:S(2)}, u32[]{:S(2)}) async-start(bf16[32,2,512]{2,1,0:T(2,128)(2,1)} %reshape.172), calls=%async_computation | async-start | bytes 131072 | tf_op jit(solution)/shard_map/all_to_all | solution.py:36
  57.4 4.0 %copy-start.1 = (bf16[512,512]{1,0:T(8,128)(2,1)S(1)}, bf16[512,512]{1,0:T(8,128)(2,1)}, u32[]{:S(2)}) copy-start(bf16[512,512]{1,0:T(8,128)(2,1)} %param.15) | copy-start | bytes 1572868
  57.4 4.0 %copy-start.4 = (f32[512]{0:T(512)S(1)}, f32[512]{0:T(512)}, u32[]{:S(2)}) copy-start(f32[512]{0:T(512)} %param.16) | copy-start | bytes 6148
  113.5 11.1 %all-to-all-start.1 = ((bf16[32,2,512]{2,1,0:T(2,128)(2,1)}), bf16[32,2,512]{2,1,0:T(2,128)(2,1)S(1)}, u32[]{:S(2)}, u32[]{:S(2)}) async-start(bf16[32,2,512]{2,1,0:T(2,128)(2,1)} %reshape.174), calls=%async_computation.1 | async-start | bytes 131072 | tf_op jit(solution)/shard_map/all_to_all | solution.py:36
  177.3 17.1 %copy-start.3 = (f32[16,512]{1,0:T(8,128)}, f32[16,512]{1,0:T(8,128)S(1)}, u32[]{:S(2)}) copy-start(f32[16,512]{1,0:T(8,128)S(1)} %fusion.13) | copy-start | bytes 98308
  177.3 14.4 %copy-start.2 = (f32[16,512]{1,0:T(8,128)S(1)}, f32[16,512]{1,0:T(8,128)}, u32[]{:S(2)}) copy-start(f32[16,512]{1,0:T(8,128)} %param.10) | copy-start | bytes 98308
  180.0 11.1 %all-to-all-start.2 = ((bf16[32,2,512]{2,1,0:T(2,128)(2,1)}), bf16[32,2,512]{2,1,0:T(2,128)(2,1)S(1)}, u32[]{:S(2)}, u32[]{:S(2)}) async-start(bf16[32,2,512]{2,1,0:T(2,128)(2,1)} %reshape.176), calls=%async_computation.2 | async-start | bytes 131072 | tf_op jit(solution)/shard_map/all_to_all | solution.py:36
where the time goes:
time: 195 us; the launch traced here: 194 us
  blocking collectives  119 us (61%)
  other arithmetic  22.4 us (11%)
  waiting for transfers between devices  17.5 us (9%)
  matrix products  14.9 us (8%)
  starting transfers between devices  11.8 us (6%)
  local copies, waits for them, and re-layouts  7.82 us (4%)
    psum x2, blocking collectives, on_device(): lax.psum((gram_of(next_vectors, stacked), gram_of(next_vectors, next_vect...  76.9 us
    psum x1, blocking collectives, on_device(): start_gram = lax.psum(gram_of(right_sides, right_sides), ('col', 'sub'))  42.1 us
    all_to_all x3, waiting for transfers between devices, apply_matrix(): lax.all_to_all(shaped, ('col', 'sub'), split_axis=0, concat_axis=1, tiled...  17.5 us
    all_to_all x3, starting transfers between devices, apply_matrix(): lax.all_to_all(shaped, ('col', 'sub'), split_axis=0, concat_axis=1, tiled...  11.8 us
    dot_general x3, matrix products, apply_matrix(): jnp.einsum('ktjr,kjnr->nkt', left_tiles, received, preferred_element_type...  6.65 us
    unnamed x17, local copies, waits for them, and re-layouts  6.14 us
    another operation x6, other arithmetic, on_device(): factor_low = jnp.linalg.cholesky(new_gram)  4.28 us
  transfers between devices with their start and end apart: 3, of which 3 were waited for; matrix products, arithmetic and copies ran while one was open for 2% of the time, Pallas kernels for 0%

commit v1 on v0

v1 whole, which is shorter than its diff:
```python
import functools

import jax
import jax.numpy as jnp
from jax import lax
from jax.experimental import pallas as pl
from jax.experimental.pallas import tpu as pltpu
from jax.sharding import PartitionSpec as P

MESH = pl.DeviceIdType.MESH
SHIFT = 2.0
highest = lax.Precision.HIGHEST


def dot_rows(first, second, precision=None):
    return lax.dot_general(
        first, second, (((1,), (1,)), ((), ())),
        preferred_element_type=jnp.float32, precision=precision,
    )


def split_rows(values):
    high = values.astype(jnp.bfloat16)
    low = (values - high.astype(jnp.float32)).astype(jnp.bfloat16)
    return jnp.concatenate([high, low], axis=0)


def join_rows(product):
    half = product.shape[0] // 2
    return product[:half] + product[half:]


def kernel(
    sub_count, tiles, chunk,
    rhs_ref, scales_ref, ranks_ref, diag_ref, right_hbm, left_hbm, near_hbm,
    sol_ref, res_ref,
    right, left, near, coeff_out, coeff_in, gram_out, gram_in, gathered,
    load_sem, send_sem, recv_sem,
):
    me = lax.axis_index("col") * sub_count + lax.axis_index("sub")
    chunks = right.shape[0] // chunk
    right_loads = []
    for c in range(chunks):
        rows = pl.ds(c * chunk, chunk)
        right_loads.append(
            pltpu.make_async_copy(right_hbm.at[rows], right.at[rows], load_sem.at[c])
        )
    near_load = pltpu.make_async_copy(near_hbm, near, load_sem.at[chunks])
    left_load = pltpu.make_async_copy(left_hbm, left, load_sem.at[chunks + 1])
    for load in right_loads:
        load.start()
    near_load.start()
    left_load.start()

    barrier = pltpu.get_barrier_semaphore()

    def partner(step):
        other = lax.rem(me + step, tiles)
        return other, (other // sub_count, lax.rem(other, sub_count))

    def greet(step, carry):
        pl.semaphore_signal(barrier, inc=1, device_id=partner(step)[1], device_id_type=MESH)
        return carry

    lax.fori_loop(1, tiles, greet, 0)

    lane = lax.broadcasted_iota(jnp.int32, (8, 128), 1)
    in_first = lane < 64

    def swap(block):
        return pltpu.roll(block, 64, 1)

    ranks = ranks_ref[...]
    keep = lax.broadcasted_iota(jnp.int32, scales_ref.shape, 1) < ranks
    weights = jnp.where(keep, scales_ref[...], 0.0)

    def project(stacked, phase, first):
        for c in range(chunks):
            if first:
                right_loads[c].wait()
            product = join_rows(dot_rows(stacked, right[pl.ds(c * chunk, chunk)]))
            for m in range(chunk // 128):
                i = c * (chunk // 64) + 2 * m
                pair = product[:, m * 128:(m + 1) * 128]
                pair = pair * jnp.concatenate([weights[i:i + 1], weights[i + 1:i + 2]], axis=1)
                upper, lower = pair[:8], pair[8:]
                coeff_out[phase, i] = jnp.where(in_first, upper, swap(lower))
                coeff_out[phase, i + 1] = jnp.where(in_first, swap(upper), lower)

    def send_coefficients(phase):
        def send(step, carry):
            other, where = partner(step)
            pltpu.make_async_remote_copy(
                src_ref=coeff_out.at[phase, other],
                dst_ref=coeff_in.at[phase, me],
                send_sem=send_sem.at[phase],
                recv_sem=recv_sem.at[phase],
                device_id=where,
                device_id_type=MESH,
            ).start()
            return carry

        lax.fori_loop(1, tiles, send, 0)
        coeff_in[phase, me] = coeff_out[phase, me]

    def send_gram(which):
        def send(step, carry):
            where = partner(step)[1]
            pltpu.make_async_remote_copy(
                src_ref=gram_out.at[which],
                dst_ref=gram_in.at[which, me],
                send_sem=send_sem.at[2 + which],
                recv_sem=recv_sem.at[2 + which],
                device_id=where,
                device_id_type=MESH,
            ).start()
            return carry

        lax.fori_loop(1, tiles, send, 0)
        gram_in[which, me] = gram_out[which]

    def all_of(buffer, index, slot):
        blocks = buffer.at[index, pl.ds(0, tiles - 1)]
        return pltpu.make_async_remote_copy(
            src_ref=blocks, dst_ref=blocks, send_sem=send_sem.at[slot], recv_sem=recv_sem.at[slot],
            device_id=partner(1)[1], device_id_type=MESH,
        )

    def far_field(phase):
        for m in range(tiles // 2):
            even, odd = coeff_in[phase, 2 * m], coeff_in[phase, 2 * m + 1]
            upper = jnp.where(in_first, even, swap(odd))
            lower = jnp.where(in_first, swap(even), odd)
            gathered[:, m * 128:(m + 1) * 128] = split_rows(jnp.concatenate([upper, lower], axis=0))
        return join_rows(dot_rows(gathered[...], left[...]))

    rhs = rhs_ref[...]
    diag = diag_ref[...]
    stacked = split_rows(rhs)
    project(stacked, 0, True)
    pl.semaphore_wait(barrier, tiles - 1)
    send_coefficients(0)
    near_load.wait()
    moved = (diag - SHIFT) * rhs + join_rows(dot_rows(stacked, near[...]))
    left_load.wait()
    all_of(coeff_in, 0, 0).wait_recv()
    moved = moved + far_field(0)
    image_1 = moved + SHIFT * rhs

    stacked = split_rows(moved)
    project(stacked, 1, False)
    send_coefficients(1)
    early = dot_rows(image_1, jnp.concatenate([rhs, image_1], axis=0), highest)
    early = jnp.concatenate([early, jnp.zeros_like(early)], axis=1)
    gram_out[0] = jnp.concatenate([early[:8], early[8:]], axis=1)
    send_gram(0)
    image_2 = diag * moved + join_rows(dot_rows(stacked, near[...]))
    all_of(coeff_in, 1, 1).wait_recv()
    image_2 = image_2 + far_field(1)

    late = dot_rows(image_2, jnp.concatenate([rhs, image_1, image_2], axis=0), highest)
    cross = dot_rows(image_1, image_2, highest)
    late = jnp.concatenate([late, cross], axis=1)
    gram_out[1] = jnp.concatenate([late[:8], late[8:]], axis=1)
    send_gram(1)

    def total(which):
        all_of(gram_in, which, 2 + which).wait_recv()
        summed = jnp.sum(gram_in[which], axis=0)
        return jnp.concatenate([summed, swap(summed)], axis=0)

    early = total(0)
    late = total(1)
    top = jnp.where(
        lax.broadcasted_iota(jnp.int32, early.shape, 1) < 32, early, pltpu.roll(late, 112, 1)
    )
    system = jnp.concatenate([top, late], axis=0)
    row_at = lax.broadcasted_iota(jnp.int32, system.shape, 0)
    for k in range(32):
        pivot = system[k:k + 1, 16 + k:17 + k]
        scaled = system[k:k + 1] * (1.0 / pivot)
        system = jnp.where(row_at == k, scaled, system - system[:, 16 + k:17 + k] * scaled)
    weights_out = jnp.transpose(system)[:16, :32]

    sol_ref[...] = jnp.dot(weights_out, jnp.concatenate([rhs, moved], axis=0), precision=highest)
    res_ref[...] = rhs - jnp.dot(
        weights_out, jnp.concatenate([image_1, image_2], axis=0), precision=highest
    )
    all_of(coeff_in, 0, 0).wait_send()
    all_of(coeff_in, 1, 1).wait_send()
    all_of(gram_in, 0, 2).wait_send()
    all_of(gram_in, 1, 3).wait_send()


def on_device(
    sub_count, right_sides, left_bases, right_bases, tile_scales, tile_ranks, near_field, diagonal
):
    rhs_count, cells = right_sides.shape
    tiles, rank_len, _ = right_bases.shape
    features = tiles * rank_len
    chunk = min(512, features)
    vmem = pl.BlockSpec(memory_space=pltpu.VMEM)
    anywhere = pl.BlockSpec(memory_space=pl.ANY)
    return pl.pallas_call(
        functools.partial(kernel, sub_count, tiles, chunk),
        out_shape=[jax.ShapeDtypeStruct((rhs_count, cells), jnp.float32)] * 2,
        in_specs=[vmem] * 4 + [anywhere] * 3,
        out_specs=[vmem] * 2,
        scratch_shapes=[
            pltpu.VMEM((features, cells), jnp.bfloat16),
            pltpu.VMEM((cells, features), jnp.bfloat16),
            pltpu.VMEM((cells, cells), jnp.bfloat16),
            pltpu.VMEM((2, tiles, 8, 128), jnp.float32),
            pltpu.VMEM((2, tiles, 8, 128), jnp.float32),
            pltpu.VMEM((2, 8, 128), jnp.float32),
            pltpu.VMEM((2, tiles, 8, 128), jnp.float32),
            pltpu.VMEM((2 * rhs_count, features), jnp.bfloat16),
            pltpu.SemaphoreType.DMA((features // chunk + 2,)),
            pltpu.SemaphoreType.DMA((4,)),
            pltpu.SemaphoreType.DMA((4,)),
        ],
        compiler_params=pltpu.CompilerParams(
            collective_id=0, has_side_effects=True, vmem_limit_bytes=48 * 1024 * 1024
        ),
    )(
        right_sides,
        tile_scales.reshape(tiles, rank_len),
        tile_ranks,
        diagonal.reshape(1, cells),
        right_bases.reshape(features, cells),
        left_bases,
        near_field,
    )


def solution(mesh):
    both = ("col", "sub")
    in_specs = (
        P(None, both), P(both, None), P(None, None, both), P(None, both, None),
        P(None, both), P(both, None), P(both),
    )
    return jax.shard_map(
        functools.partial(on_device, mesh.shape["sub"]), mesh=mesh, in_specs=in_specs,
        out_specs=(P(None, both), P(None, both)), check_vma=False,
    )
```

time: 195 us -> 38.9 us (0.20)
  blocking collectives: 119 us -> 0 us
  Pallas kernels: 0 us -> 29.6 us
  other arithmetic: 22.4 us -> 0 us
  waiting for transfers between devices: 17.5 us -> 0 us
  matrix products: 14.9 us -> 0 us
  starting transfers between devices: 11.8 us -> 0 us
    psum x3 -> x0, blocking collectives: 119 us -> none  [the longest x2 76.9 us: on_device(): lax.psum((gram_of(next_vectors, stacked), gram_of(next_vectors, next_vect...]
    pallas_call x0 -> x1, Pallas kernels: none -> 29.6 us  [on_device(): pl.pallas_call(functools.partial(kernel, sub_count, tiles, chunk), out_sh...]
    all_to_all x3 -> x0, waiting for transfers between devices: 17.5 us -> none  [apply_matrix(): lax.all_to_all(shaped, ('col', 'sub'), split_axis=0, concat_axis=1, tiled...]
    another operation x18 -> x0, other arithmetic: 16.8 us -> none  [the longest x6 4.28 us: on_device(): factor_low = jnp.linalg.cholesky(new_gram)]
    dot_general x20 -> x0, matrix products: 13.4 us -> none  [the longest x3 6.65 us: apply_matrix(): jnp.einsum('ktjr,kjnr->nkt', left_tiles, received, preferred_element_type...]
    all_to_all x3 -> x0, starting transfers between devices: 11.8 us -> none  [apply_matrix(): lax.all_to_all(shaped, ('col', 'sub'), split_axis=0, concat_axis=1, tiled...]
    reshape x3 -> x0, other arithmetic: 2.94 us -> none  [apply_matrix(): shaped = coefficients.reshape(total_tiles, local_tiles, feature_len)]
    unnamed x17 -> x15, local copies, waits for them, and re-layouts: 6.14 us -> 8.35 us
  transfers between devices with their start and end apart: 3 -> 0, of which waited for: 3 -> 0; matrix products, arithmetic and copies ran while one was open for 2% -> 0% of each run, Pallas kernels for 0% -> 0%
where the time goes in v1:
time: 38.9 us; the launch traced here: 38.6 us
  Pallas kernels  29.6 us (76%)
  local copies, waits for them, and re-layouts  8.35 us (21%)
  between operations  0.64 us (2%)
    pallas_call x1, Pallas kernels, on_device(): pl.pallas_call(functools.partial(kernel, sub_count, tiles, chunk), out_sh...  29.6 us
    unnamed x15, local copies, waits for them, and re-layouts  8.35 us

profile of v1, /device:TPU:0, one launch (start us, length us, event | category | flops | bytes accessed | tf_op | source)
XLA Modules:
  0.0 38.6 jit_solution(6557147160991488549)
XLA Ops:
  0.6 0.7 %copy.9.ranks_ref = s32[32,1]{1,0:T(8,128)S(1)} copy(s32[32,1]{0,1:T(1,128)} %param.11) | data formatting | bytes 256 | tf_op args[4]
  1.4 0.0 copy-start
  1.4 1.6 %copy-done = bf16[32,64,512]{2,1,0:T(8,128)(2,1)S(1)} copy-done((bf16[32,64,512]{2,1,0:T(8,128)(2,1)S(1)}, bf16[32,64,512]{2,1,0:T(8,128)(2,1)}, u32[]{:S(2)}) %copy-start) | copy-done | bytes 2097176
  3.0 0.0 copy-start.1
  3.0 1.6 %copy-done.1 = bf16[512,2048]{1,0:T(8,128)(2,1)S(1)} copy-done((bf16[512,2048]{1,0:T(8,128)(2,1)S(1)}, bf16[512,2048]{1,0:T(8,128)(2,1)}, u32[]{:S(2)}) %copy-start.1) | copy-done | bytes 2097176
  4.5 0.0 copy-start.2
  4.6 1.0 %copy-done.2 = bf16[512,512]{1,0:T(8,128)(2,1)S(1)} copy-done((bf16[512,512]{1,0:T(8,128)(2,1)S(1)}, bf16[512,512]{1,0:T(8,128)(2,1)}, u32[]{:S(2)}) %copy-start.2) | copy-done | bytes 524312
  5.6 0.0 copy-start.3
  5.6 0.8 %copy-done.3 = f32[16,512]{1,0:T(8,128)S(1)} copy-done((f32[16,512]{1,0:T(8,128)S(1)}, f32[16,512]{1,0:T(8,128)}, u32[]{:S(2)}) %copy-start.3) | copy-done | bytes 32792
  6.3 0.0 copy-start.4
  6.4 0.7 %copy-done.4 = f32[32,1,64]{2,1,0:T(1,128)S(1)} copy-done((f32[32,1,64]{2,1,0:T(1,128)S(1)}, f32[32,1,64]{2,1,0:T(1,128)}, u32[]{:S(2)}) %copy-start.4) | copy-done | bytes 8216
  7.1 0.0 copy-start.5
  7.1 0.7 %copy-done.5 = f32[512]{0:T(512)S(1)} copy-done((f32[512]{0:T(512)S(1)}, f32[512]{0:T(512)}, u32[]{:S(2)}) %copy-start.5) | copy-done | bytes 2072
  7.8 29.6 %shard_map.86 = (f32[16,512]{1,0:T(8,128)S(1)}, f32[16,512]{1,0:T(8,128)S(1)}) custom-call(f32[16,512]{1,0:T(8,128)S(1)} %copy-done.3, f32[32,64]{1,0:T(8,128)S(1)} %bitcast.4, s32[32,1]{1,0:T(8,128)S(1)} %copy.9.ranks_ref, f32[1,512]{1,0:T(1,128)S(1)} %bitcast.5, bf16[2048,512]{1,0:T(8,128)(2,1)S(1)} %bitcast.3, bf16[512,2048]{1,0:T(8,128)(2,1)S(1)} %copy-done.1, ...), custom_call_target="tpu_custom_call" | custom-call | tf_op jit(solution)/shard_map/pallas_call | solution.py:204
  37.3 0.6 %copy.12 = f32[16,512]{1,0:T(8,128)} copy(f32[16,512]{1,0:T(8,128)S(1)} %get-tuple-element.4) | data formatting | bytes 65536
  37.9 0.6 %copy.13 = f32[16,512]{1,0:T(8,128)} copy(f32[16,512]{1,0:T(8,128)S(1)} %get-tuple-element.5) | data formatting | bytes 65536
Async XLA Ops:
  1.4 1.6 %copy-start = (bf16[32,64,512]{2,1,0:T(8,128)(2,1)S(1)}, bf16[32,64,512]{2,1,0:T(8,128)(2,1)}, u32[]{:S(2)}) copy-start(bf16[32,64,512]{2,1,0:T(8,128)(2,1)} %param.9) | copy-start | bytes 6291460
  3.0 1.6 %copy-start.1 = (bf16[512,2048]{1,0:T(8,128)(2,1)S(1)}, bf16[512,2048]{1,0:T(8,128)(2,1)}, u32[]{:S(2)}) copy-start(bf16[512,2048]{1,0:T(8,128)(2,1)} %left_hbm.1) | copy-start | bytes 6291460
  4.5 1.0 %copy-start.2 = (bf16[512,512]{1,0:T(8,128)(2,1)S(1)}, bf16[512,512]{1,0:T(8,128)(2,1)}, u32[]{:S(2)}) copy-start(bf16[512,512]{1,0:T(8,128)(2,1)} %near_hbm.1) | copy-start | bytes 1572868
  5.6 0.8 %copy-start.3 = (f32[16,512]{1,0:T(8,128)S(1)}, f32[16,512]{1,0:T(8,128)}, u32[]{:S(2)}) copy-start(f32[16,512]{1,0:T(8,128)} %rhs_ref.1) | copy-start | bytes 98308
  6.3 0.7 %copy-start.4 = (f32[32,1,64]{2,1,0:T(1,128)S(1)}, f32[32,1,64]{2,1,0:T(1,128)}, u32[]{:S(2)}) copy-start(f32[32,1,64]{2,1,0:T(1,128)} %param.10) | copy-start | bytes 24580
  7.1 0.7 %copy-start.5 = (f32[512]{0:T(512)S(1)}, f32[512]{0:T(512)}, u32[]{:S(2)}) copy-start(f32[512]{0:T(512)} %param.13) | copy-start | bytes 6148

commit v2 on v1

v2 whole, which is shorter than its diff:
```python
import functools

import jax
import jax.numpy as jnp
from jax import lax
from jax.experimental import pallas as pl
from jax.experimental.pallas import tpu as pltpu
from jax.sharding import PartitionSpec as P

MESH = pl.DeviceIdType.MESH
SHIFT = 2.0
PIVOTS = 8
VMEM_BYTES = 60 * 1024 * 1024
highest = lax.Precision.HIGHEST


def dot_rows(first, second, precision=None):
    return lax.dot_general(
        first, second, (((1,), (1,)), ((), ())),
        preferred_element_type=jnp.float32, precision=precision,
    )


def split_rows(values):
    high = values.astype(jnp.bfloat16)
    low = (values - high.astype(jnp.float32)).astype(jnp.bfloat16)
    return jnp.concatenate([high, low], axis=0)


def join_rows(product):
    half = product.shape[0] // 2
    return product[:half] + product[half:]


def kernel(
    col_count, sub_count, tiles, chunk,
    rhs_hbm, scales_hbm, ranks_hbm, diag_hbm, right_hbm, left_hbm, near_hbm,
    sol_ref, res_ref,
    rhs_ref, scales_ref, ranks_ref, diag_ref, right, left, near,
    coeff_out, coeff_in, gram_out, gram_near, gram_far, gathered,
    load_sem, send_sem, recv_sem,
):
    my_col, my_sub = lax.axis_index("col"), lax.axis_index("sub")
    me = my_col * sub_count + my_sub
    chunks = right.shape[0] // chunk
    small_loads = [
        pltpu.make_async_copy(source, target, load_sem.at[chunks + 2 + n])
        for n, (source, target) in enumerate([
            (rhs_hbm, rhs_ref), (scales_hbm, scales_ref),
            (ranks_hbm, ranks_ref), (diag_hbm, diag_ref),
        ])
    ]
    right_loads = []
    for c in range(chunks):
        rows = pl.ds(c * chunk, chunk)
        right_loads.append(
            pltpu.make_async_copy(right_hbm.at[rows], right.at[rows], load_sem.at[c])
        )
    near_load = pltpu.make_async_copy(near_hbm, near, load_sem.at[chunks])
    left_load = pltpu.make_async_copy(left_hbm, left, load_sem.at[chunks + 1])
    for load in small_loads + right_loads:
        load.start()
    near_load.start()
    left_load.start()

    barrier = pltpu.get_barrier_semaphore()
    subs = [my_sub] + [lax.rem(my_sub + step, sub_count) for step in range(1, sub_count)]

    def each_partner(act):
        for sub in subs[1:]:
            act(my_col, sub)

        def column(step, carry):
            col = lax.rem(my_col + step, col_count)
            for sub in subs:
                act(col, sub)
            return carry

        lax.fori_loop(1, col_count, column, 0)

    def greet(col, sub):
        pl.semaphore_signal(barrier, inc=1, device_id=(col, sub), device_id_type=MESH)

    each_partner(greet)

    lane = lax.broadcasted_iota(jnp.int32, (8, 128), 1)
    in_first = lane < 64

    def swap(block):
        return pltpu.roll(block, 64, 1)

    for load in small_loads:
        load.wait()
    square = (tiles, tiles)
    on_diagonal = lax.broadcasted_iota(jnp.int32, square, 0) == lax.broadcasted_iota(
        jnp.int32, square, 1
    )
    ranks = jnp.sum(jnp.where(on_diagonal, ranks_ref[...], 0), axis=1, keepdims=True)
    keep = lax.broadcasted_iota(jnp.int32, scales_ref.shape, 1) < ranks
    weights = jnp.where(keep, scales_ref[...], 0.0)

    def project(stacked, phase, first):
        for c in range(chunks):
            if first:
                right_loads[c].wait()
            product = join_rows(dot_rows(stacked, right[pl.ds(c * chunk, chunk)]))
            for m in range(chunk // 128):
                i = c * (chunk // 64) + 2 * m
                pair = product[:, m * 128:(m + 1) * 128]
                pair = pair * jnp.concatenate([weights[i:i + 1], weights[i + 1:i + 2]], axis=1)
                upper, lower = pair[:8], pair[8:]
                coeff_out[phase, i] = jnp.where(in_first, upper, swap(lower))
                coeff_out[phase, i + 1] = jnp.where(in_first, swap(upper), lower)

    def remote(source, target, slot, col, sub):
        return pltpu.make_async_remote_copy(
            src_ref=source, dst_ref=target, send_sem=send_sem.at[slot], recv_sem=recv_sem.at[slot],
            device_id=(col, sub), device_id_type=MESH,
        )

    def send_coefficients(phase):
        def send(col, sub):
            other = col * sub_count + sub
            remote(coeff_out.at[phase, other], coeff_in.at[phase, me], phase, col, sub).start()

        each_partner(send)
        coeff_in[phase, me] = coeff_out[phase, me]

    def all_of(blocks, slot):
        return remote(blocks, blocks, slot, my_col, subs[1])

    def coefficients_of(phase):
        return all_of(coeff_in.at[phase, pl.ds(0, tiles - 1)], phase)

    near_grams = all_of(gram_near.at[pl.ds(0, sub_count - 1)], 2)
    far_grams = all_of(gram_far.at[pl.ds(0, col_count - 1)], 3)

    def far_field(phase):
        for m in range(tiles // 2):
            even, odd = coeff_in[phase, 2 * m], coeff_in[phase, 2 * m + 1]
            upper = jnp.where(in_first, even, swap(odd))
            lower = jnp.where(in_first, swap(even), odd)
            gathered[:, m * 128:(m + 1) * 128] = split_rows(jnp.concatenate([upper, lower], axis=0))
        return join_rows(dot_rows(gathered[...], left[...]))

    rhs = rhs_ref[...]
    diag = diag_ref[...]
    stacked = split_rows(rhs)
    project(stacked, 0, True)
    pl.semaphore_wait(barrier, tiles - 1)
    send_coefficients(0)
    near_load.wait()
    moved = (diag - SHIFT) * rhs + join_rows(dot_rows(stacked, near[...]))
    left_load.wait()
    coefficients_of(0).wait_recv()
    moved = moved + far_field(0)
    image_1 = moved + SHIFT * rhs

    stacked = split_rows(moved)
    project(stacked, 1, False)
    send_coefficients(1)
    early = dot_rows(image_1, jnp.concatenate([rhs, image_1], axis=0), highest)
    early = jnp.concatenate([early, jnp.zeros_like(early)], axis=1)
    gram_out[0, :8] = jnp.concatenate([early[:8], early[8:]], axis=1)
    image_2 = diag * moved + join_rows(dot_rows(stacked, near[...]))
    coefficients_of(1).wait_recv()
    image_2 = image_2 + far_field(1)

    late = dot_rows(image_2, jnp.concatenate([rhs, image_1, image_2], axis=0), highest)
    cross = dot_rows(image_1, image_2, highest)
    late = jnp.concatenate([late, cross], axis=1)
    gram_out[0, 8:] = jnp.concatenate([late[:8], late[8:]], axis=1)

    for sub in subs[1:]:
        remote(gram_out.at[0], gram_near.at[my_sub], 2, my_col, sub).start()
    gram_near[my_sub] = gram_out[0]
    near_grams.wait_recv()
    gram_out[1] = jnp.sum(gram_near[...], axis=0)
    for step in range(1, col_count):
        col = lax.rem(my_col + step, col_count)
        remote(gram_out.at[1], gram_far.at[my_col], 3, col, my_sub).start()
    gram_far[my_col] = gram_out[1]
    far_grams.wait_recv()
    summed = jnp.sum(gram_far[...], axis=0)

    def unfold(block):
        return jnp.concatenate([block, swap(block)], axis=0)

    early, late = unfold(summed[:8]), unfold(summed[8:])
    top = jnp.where(
        lax.broadcasted_iota(jnp.int32, early.shape, 1) < 32, early, pltpu.roll(late, 112, 1)
    )
    system = jnp.concatenate([top, late], axis=0)
    row_at = lax.broadcasted_iota(jnp.int32, system.shape, 0)
    for start in range(0, 32, PIVOTS):
        columns = [
            jnp.broadcast_to(system[:, 16 + k:17 + k], system.shape)
            for k in range(start, start + PIVOTS)
        ]
        for n in range(PIVOTS):
            k = start + n
            factors = columns[n]
            inverse = 1.0 / factors[k:k + 1]

            def eliminate(block):
                scaled = block[k:k + 1] * inverse
                return jnp.where(row_at == k, scaled, block - factors * scaled)

            columns[n + 1:] = [eliminate(column) for column in columns[n + 1:]]
            system = eliminate(system)
    weights_out = jnp.transpose(system)[:16, :32]

    sol_ref[...] = jnp.dot(weights_out, jnp.concatenate([rhs, moved], axis=0), precision=highest)
    res_ref[...] = rhs - jnp.dot(
        weights_out, jnp.concatenate([image_1, image_2], axis=0), precision=highest
    )
    coefficients_of(0).wait_send()
    coefficients_of(1).wait_send()
    near_grams.wait_send()
    far_grams.wait_send()


def on_device(
    col_count, sub_count, right_sides, left_bases, right_bases, tile_scales, tile_ranks, near_field,
    diagonal,
):
    rhs_count, cells = right_sides.shape
    tiles, rank_len, _ = right_bases.shape
    features = tiles * rank_len
    chunk = min(512, features)
    vmem = pl.BlockSpec(memory_space=pltpu.VMEM)
    anywhere = pl.BlockSpec(memory_space=pl.ANY)
    return pl.pallas_call(
        functools.partial(kernel, col_count, sub_count, tiles, chunk),
        out_shape=[jax.ShapeDtypeStruct((rhs_count, cells), jnp.float32)] * 2,
        in_specs=[anywhere] * 7,
        out_specs=[vmem] * 2,
        scratch_shapes=[
            pltpu.VMEM((rhs_count, cells), jnp.float32),
            pltpu.VMEM((tiles, rank_len), jnp.float32),
            pltpu.VMEM((1, tiles), jnp.int32),
            pltpu.VMEM((1, cells), jnp.float32),
            pltpu.VMEM((features, cells), jnp.bfloat16),
            pltpu.VMEM((cells, features), jnp.bfloat16),
            pltpu.VMEM((cells, cells), jnp.bfloat16),
            pltpu.VMEM((2, tiles, 8, 128), jnp.float32),
            pltpu.VMEM((2, tiles, 8, 128), jnp.float32),
            pltpu.VMEM((2, 16, 128), jnp.float32),
            pltpu.VMEM((sub_count, 16, 128), jnp.float32),
            pltpu.VMEM((col_count, 16, 128), jnp.float32),
            pltpu.VMEM((2 * rhs_count, features), jnp.bfloat16),
            pltpu.SemaphoreType.DMA((features // chunk + 6,)),
            pltpu.SemaphoreType.DMA((4,)),
            pltpu.SemaphoreType.DMA((4,)),
        ],
        compiler_params=pltpu.CompilerParams(
            collective_id=0, has_side_effects=True, vmem_limit_bytes=VMEM_BYTES
        ),
    )(
        right_sides,
        tile_scales.reshape(tiles, rank_len),
        tile_ranks.reshape(1, tiles),
        diagonal.reshape(1, cells),
        right_bases.reshape(features, cells),
        left_bases,
        near_field,
    )


def solution(mesh):
    both = ("col", "sub")
    in_specs = (
        P(None, both), P(both, None), P(None, None, both), P(None, both, None),
        P(None, both), P(both, None), P(both),
    )
    return jax.shard_map(
        functools.partial(on_device, mesh.shape["col"], mesh.shape["sub"]), mesh=mesh, in_specs=in_specs,
        out_specs=(P(None, both), P(None, both)), check_vma=False,
    )
```

time: 38.9 us -> 32.4 us (0.83)
  local copies, waits for them, and re-layouts: 8.35 us -> 2.75 us
  Pallas kernels: 29.6 us -> 28.7 us
    unnamed x15 -> x2, local copies, waits for them, and re-layouts: 8.35 us -> 2.75 us
    pallas_call x1, Pallas kernels: 29.6 us -> 28.7 us  [on_device(): pl.pallas_call(functools.partial(kernel, col_count, sub_count, tiles, chu...]
where the time goes in v2:
time: 32.4 us; the launch traced here: 32.1 us
  Pallas kernels  28.7 us (89%)
  local copies, waits for them, and re-layouts  2.75 us (8%)
  between operations  0.64 us (2%)
    pallas_call x1, Pallas kernels, on_device(): pl.pallas_call(functools.partial(kernel, col_count, sub_count, tiles, chu...  28.7 us
    unnamed x2, local copies, waits for them, and re-layouts  2.75 us

profile of v2, /device:TPU:0, one launch (start us, length us, event | category | flops | bytes accessed | tf_op | source)
XLA Modules:
  0.0 32.1 jit_solution(1361652754633841588)
XLA Ops:
  0.6 28.7 %shard_map.86 = (f32[16,512]{1,0:T(8,128)}, f32[16,512]{1,0:T(8,128)}) custom-call(f32[16,512]{1,0:T(8,128)} %rhs_hbm.1, f32[32,64]{1,0:T(8,128)} %bitcast.5, s32[1,32]{1,0:T(1,128)} %bitcast.7, f32[1,512]{1,0:T(1,128)} %bitcast.6, bf16[2048,512]{1,0:T(8,128)(2,1)} %bitcast.4, bf16[512,2048]{1,0:T(8,128)(2,1)} %left_hbm.1, bf16[512,512]{1,0:T(8,128)(2,1)} %near_hbm.1), custom_call_target="tpu_custom_call" | custom-call | tf_op jit(solution)/shard_map/pallas_call | solution.py:233
  29.4 1.4 %copy.11 = f32[16,512]{1,0:T(8,128)} copy(f32[16,512]{1,0:T(8,128)} %get-tuple-element.4) | data formatting | bytes 65536
  30.7 1.4 %copy.12 = f32[16,512]{1,0:T(8,128)} copy(f32[16,512]{1,0:T(8,128)} %get-tuple-element.5) | data formatting | bytes 65536

commit v3 on v2

--- a/solution.py
+++ b/solution.py
@@ -35,9 +35,9 @@
 def kernel(
     col_count, sub_count, tiles, chunk,
     rhs_hbm, scales_hbm, ranks_hbm, diag_hbm, right_hbm, left_hbm, near_hbm,
-    sol_ref, res_ref,
-    rhs_ref, scales_ref, ranks_ref, diag_ref, right, left, near,
-    coeff_out, coeff_in, gram_out, gram_near, gram_far, gathered,
+    vectors_hbm, system_hbm,
+    rhs_ref, scales_ref, ranks_ref, diag_ref, right, left, near, vectors, system_ref,
+    coeff_out, coeff_in, gram_out, gram_in, gathered,
     load_sem, send_sem, recv_sem,
 ):
     my_col, my_sub = lax.axis_index("col"), lax.axis_index("sub")
@@ -132,8 +132,17 @@
     def coefficients_of(phase):
         return all_of(coeff_in.at[phase, pl.ds(0, tiles - 1)], phase)
 
-    near_grams = all_of(gram_near.at[pl.ds(0, sub_count - 1)], 2)
-    far_grams = all_of(gram_far.at[pl.ds(0, col_count - 1)], 3)
+    def grams_of(which):
+        return all_of(gram_in.at[which, pl.ds(0, tiles - 1)], 2 + which)
+
+    def send_gram(which, block):
+        gram_out[which] = jnp.concatenate([block[:8], block[8:]], axis=1)
+
+        def send(col, sub):
+            remote(gram_out.at[which], gram_in.at[which, me], 2 + which, col, sub).start()
+
+        each_partner(send)
+        gram_in[which, me] = gram_out[which]
 
     def far_field(phase):
         for m in range(tiles // 2):
@@ -156,37 +165,39 @@
     moved = moved + far_field(0)
     image_1 = moved + SHIFT * rhs
 
+    count = rhs.shape[0]
+    vectors[:count] = moved
+    vectors[count:2 * count] = image_1
+    first_store = pltpu.make_async_copy(
+        vectors.at[pl.ds(0, 2 * count)], vectors_hbm.at[pl.ds(0, 2 * count)],
+        load_sem.at[chunks + 6],
+    )
+    first_store.start()
     stacked = split_rows(moved)
     project(stacked, 1, False)
     send_coefficients(1)
     early = dot_rows(image_1, jnp.concatenate([rhs, image_1], axis=0), highest)
-    early = jnp.concatenate([early, jnp.zeros_like(early)], axis=1)
-    gram_out[0, :8] = jnp.concatenate([early[:8], early[8:]], axis=1)
+    send_gram(0, jnp.concatenate([early, jnp.zeros_like(early)], axis=1))
     image_2 = diag * moved + join_rows(dot_rows(stacked, near[...]))
     coefficients_of(1).wait_recv()
     image_2 = image_2 + far_field(1)
 
+    vectors[2 * count:] = image_2
+    second_store = pltpu.make_async_copy(
+        vectors.at[pl.ds(2 * count, count)], vectors_hbm.at[pl.ds(2 * count, count)],
+        load_sem.at[chunks + 7],
+    )
+    second_store.start()
     late = dot_rows(image_2, jnp.concatenate([rhs, image_1, image_2], axis=0), highest)
     cross = dot_rows(image_1, image_2, highest)
-    late = jnp.concatenate([late, cross], axis=1)
-    gram_out[0, 8:] = jnp.concatenate([late[:8], late[8:]], axis=1)
-
-    for sub in subs[1:]:
-        remote(gram_out.at[0], gram_near.at[my_sub], 2, my_col, sub).start()
-    gram_near[my_sub] = gram_out[0]
-    near_grams.wait_recv()
-    gram_out[1] = jnp.sum(gram_near[...], axis=0)
-    for step in range(1, col_count):
-        col = lax.rem(my_col + step, col_count)
-        remote(gram_out.at[1], gram_far.at[my_col], 3, col, my_sub).start()
-    gram_far[my_col] = gram_out[1]
-    far_grams.wait_recv()
-    summed = jnp.sum(gram_far[...], axis=0)
-
-    def unfold(block):
-        return jnp.concatenate([block, swap(block)], axis=0)
-
-    early, late = unfold(summed[:8]), unfold(summed[8:])
+    send_gram(1, jnp.concatenate([late, cross], axis=1))
+
+    def total(which):
+        grams_of(which).wait_recv()
+        summed = jnp.sum(gram_in[which], axis=0)
+        return jnp.concatenate([summed, swap(summed)], axis=0)
+
+    early, late = total(0), total(1)
     top = jnp.where(
         lax.broadcasted_iota(jnp.int32, early.shape, 1) < 32, early, pltpu.roll(late, 112, 1)
     )
@@ -208,16 +219,25 @@
 
             columns[n + 1:] = [eliminate(column) for column in columns[n + 1:]]
             system = eliminate(system)
-    weights_out = jnp.transpose(system)[:16, :32]
-
-    sol_ref[...] = jnp.dot(weights_out, jnp.concatenate([rhs, moved], axis=0), precision=highest)
-    res_ref[...] = rhs - jnp.dot(
-        weights_out, jnp.concatenate([image_1, image_2], axis=0), precision=highest
-    )
+    system_ref[...] = system
+    last_store = pltpu.make_async_copy(system_ref, system_hbm, load_sem.at[chunks + 8])
+    last_store.start()
     coefficients_of(0).wait_send()
     coefficients_of(1).wait_send()
-    near_grams.wait_send()
-    far_grams.wait_send()
+    grams_of(0).wait_send()
+    grams_of(1).wait_send()
+    first_store.wait()
+    second_store.wait()
+    last_store.wait()
+
+
+def combine(rhs_ref, vectors_ref, system_ref, sol_ref, res_ref):
+    rhs = rhs_ref[...]
+    count = rhs.shape[0]
+    mix = jnp.transpose(system_ref[...])[:count, :2 * count]
+    basis = jnp.concatenate([rhs, vectors_ref[:count]], axis=0)
+    sol_ref[...] = jnp.dot(mix, basis, precision=highest)
+    res_ref[...] = rhs - jnp.dot(mix, vectors_ref[count:], precision=highest)
 
 
 def on_device(
@@ -230,11 +250,14 @@
     chunk = min(512, features)
     vmem = pl.BlockSpec(memory_space=pltpu.VMEM)
     anywhere = pl.BlockSpec(memory_space=pl.ANY)
-    return pl.pallas_call(
+    vectors, system = pl.pallas_call(
         functools.partial(kernel, col_count, sub_count, tiles, chunk),
-        out_shape=[jax.ShapeDtypeStruct((rhs_count, cells), jnp.float32)] * 2,
+        out_shape=[
+            jax.ShapeDtypeStruct((3 * rhs_count, cells), jnp.float32),
+            jax.ShapeDtypeStruct((2 * rhs_count, 128), jnp.float32),
+        ],
         in_specs=[anywhere] * 7,
-        out_specs=[vmem] * 2,
+        out_specs=[anywhere] * 2,
         scratch_shapes=[
             pltpu.VMEM((rhs_count, cells), jnp.float32),
             pltpu.VMEM((tiles, rank_len), jnp.float32),
@@ -243,13 +266,14 @@
             pltpu.VMEM((features, cells), jnp.bfloat16),
             pltpu.VMEM((cells, features), jnp.bfloat16),
             pltpu.VMEM((cells, cells), jnp.bfloat16),
+            pltpu.VMEM((3 * rhs_count, cells), jnp.float32),
+            pltpu.VMEM((2 * rhs_count, 128), jnp.float32),
             pltpu.VMEM((2, tiles, 8, 128), jnp.float32),
             pltpu.VMEM((2, tiles, 8, 128), jnp.float32),
-            pltpu.VMEM((2, 16, 128), jnp.float32),
-            pltpu.VMEM((sub_count, 16, 128), jnp.float32),
-            pltpu.VMEM((col_count, 16, 128), jnp.float32),
+            pltpu.VMEM((2, 8, 128), jnp.float32),
+            pltpu.VMEM((2, tiles, 8, 128), jnp.float32),
             pltpu.VMEM((2 * rhs_count, features), jnp.bfloat16),
-            pltpu.SemaphoreType.DMA((features // chunk + 6,)),
+            pltpu.SemaphoreType.DMA((features // chunk + 9,)),
             pltpu.SemaphoreType.DMA((4,)),
             pltpu.SemaphoreType.DMA((4,)),
         ],
@@ -265,6 +289,13 @@
         left_bases,
         near_field,
     )
+    return pl.pallas_call(
+        combine,
+        out_shape=[jax.ShapeDtypeStruct((rhs_count, cells), jnp.float32)] * 2,
+        in_specs=[vmem] * 3,
+        out_specs=[vmem] * 2,
+        compiler_params=pltpu.CompilerParams(vmem_limit_bytes=VMEM_BYTES),
+    )(right_sides, vectors, system)
 
 
 def solution(mesh):

time: 32.4 us -> 30.9 us (0.954)
  local copies, waits for them, and re-layouts: 2.75 us -> 0 us
  Pallas kernels: 28.7 us -> 30.1 us
    unnamed x2 -> x0, local copies, waits for them, and re-layouts: 2.75 us -> none
    pallas_call x0 -> x1, Pallas kernels: none -> 1.78 us  [on_device(): pl.pallas_call(combine, out_shape=[jax.ShapeDtypeStruct((rhs_count, cells...]
    pallas_call x1, Pallas kernels: 28.7 us -> 28.3 us  [on_device(): pl.pallas_call(functools.partial(kernel, col_count, sub_count, tiles, chu...]
where the time goes in v3:
time: 30.9 us; the launch traced here: 30.7 us
  Pallas kernels  30.1 us (97%)
  between operations  0.64 us (2%)
    pallas_call x1, Pallas kernels, on_device(): pl.pallas_call(functools.partial(kernel, col_count, sub_count, tiles, chu...  28.3 us
    pallas_call x1, Pallas kernels, on_device(): pl.pallas_call(combine, out_shape=[jax.ShapeDtypeStruct((rhs_count, cells...  1.78 us

profile of v3, /device:TPU:0, one launch (start us, length us, event | category | flops | bytes accessed | tf_op | source)
XLA Modules:
  0.0 30.7 jit_solution(6086644791865383232)
XLA Ops:
  0.6 28.3 %shard_map.86 = (f32[48,512]{1,0:T(8,128)}, f32[32,128]{1,0:T(8,128)}) custom-call(f32[16,512]{1,0:T(8,128)} %rhs_ref.1, f32[32,64]{1,0:T(8,128)} %bitcast.5, s32[1,32]{1,0:T(1,128)} %bitcast.7, f32[1,512]{1,0:T(1,128)} %bitcast.6, bf16[2048,512]{1,0:T(8,128)(2,1)} %bitcast.4, bf16[512,2048]{1,0:T(8,128)(2,1)} %left_hbm.1, bf16[512,512]{1,0:T(8,128)(2,1)} %near_hbm.1), custom_call_target="tpu_custom_call" | custom-call | tf_op jit(solution)/shard_map/pallas_call | solution.py:253
  28.9 1.8 %shard_map.87 = (f32[16,512]{1,0:T(8,128)}, f32[16,512]{1,0:T(8,128)}) custom-call(f32[16,512]{1,0:T(8,128)} %rhs_ref.1, f32[48,512]{1,0:T(8,128)} %get-tuple-element.4.vectors_ref, f32[32,128]{1,0:T(8,128)} %get-tuple-element.5.system_ref), custom_call_target="tpu_custom_call" | custom-call | tf_op jit(solution)/shard_map/pallas_call | solution.py:292

commit v4 on v3

--- a/solution.py
+++ b/solution.py
@@ -37,7 +37,7 @@
     rhs_hbm, scales_hbm, ranks_hbm, diag_hbm, right_hbm, left_hbm, near_hbm,
     vectors_hbm, system_hbm,
     rhs_ref, scales_ref, ranks_ref, diag_ref, right, left, near, vectors, system_ref,
-    coeff_out, coeff_in, gram_out, gram_in, gathered,
+    coeff_out, coeff_in, gram_out, gram_in, pair_weights,
     load_sem, send_sem, recv_sem,
 ):
     my_col, my_sub = lax.axis_index("col"), lax.axis_index("sub")
@@ -50,9 +50,18 @@
             (ranks_hbm, ranks_ref), (diag_hbm, diag_ref),
         ])
     ]
+    group_tiles = chunk // 64
+    group_cols = group_tiles // sub_count
+    my_group = my_col // group_cols
+    groups = [my_group] + [lax.rem(my_group + k, chunks) for k in range(1, chunks)]
+    outward = list(range(1, chunks)) + [0]
+
+    def span(k):
+        return pl.ds(pl.multiple_of(groups[k] * chunk, chunk), chunk)
+
     right_loads = []
-    for c in range(chunks):
-        rows = pl.ds(c * chunk, chunk)
+    for c in outward:
+        rows = span(c)
         right_loads.append(
             pltpu.make_async_copy(right_hbm.at[rows], right.at[rows], load_sem.at[c])
         )
@@ -99,32 +108,41 @@
     keep = lax.broadcasted_iota(jnp.int32, scales_ref.shape, 1) < ranks
     weights = jnp.where(keep, scales_ref[...], 0.0)
 
-    def project(stacked, phase, first):
-        for c in range(chunks):
-            if first:
-                right_loads[c].wait()
-            product = join_rows(dot_rows(stacked, right[pl.ds(c * chunk, chunk)]))
-            for m in range(chunk // 128):
-                i = c * (chunk // 64) + 2 * m
-                pair = product[:, m * 128:(m + 1) * 128]
-                pair = pair * jnp.concatenate([weights[i:i + 1], weights[i + 1:i + 2]], axis=1)
-                upper, lower = pair[:8], pair[8:]
-                coeff_out[phase, i] = jnp.where(in_first, upper, swap(lower))
-                coeff_out[phase, i + 1] = jnp.where(in_first, swap(upper), lower)
-
-    def remote(source, target, slot, col, sub):
+    for m in range(tiles // 2):
+        pair_weights[m:m + 1] = jnp.concatenate(
+            [weights[2 * m:2 * m + 1], weights[2 * m + 1:2 * m + 2]], axis=1
+        )
+
+    def project(stacked, phase, k):
+        product = join_rows(dot_rows(stacked, right[span(k)]))
+        for m in range(chunk // 128):
+            at = groups[k] * (group_tiles // 2) + m
+            pair = product[:, m * 128:(m + 1) * 128] * pair_weights[pl.ds(at, 1)]
+            upper, lower = pair[:8], pair[8:]
+            coeff_out[phase, 2 * at] = jnp.where(in_first, upper, swap(lower))
+            coeff_out[phase, 2 * at + 1] = jnp.where(in_first, swap(upper), lower)
+
+    def remote(source, target, slot, col, sub, arrival=None):
         return pltpu.make_async_remote_copy(
-            src_ref=source, dst_ref=target, send_sem=send_sem.at[slot], recv_sem=recv_sem.at[slot],
+            src_ref=source, dst_ref=target, send_sem=send_sem.at[slot],
+            recv_sem=recv_sem.at[slot if arrival is None else arrival],
             device_id=(col, sub), device_id_type=MESH,
         )
 
-    def send_coefficients(phase):
-        def send(col, sub):
-            other = col * sub_count + sub
-            remote(coeff_out.at[phase, other], coeff_in.at[phase, me], phase, col, sub).start()
-
-        each_partner(send)
-        coeff_in[phase, me] = coeff_out[phase, me]
+    def arrival_of(phase, group):
+        return 4 + phase * chunks + group
+
+    def send_group(phase, k):
+        for a in range(group_cols):
+            col = groups[k] * group_cols + lax.rem(my_col + a, group_cols)
+            for b, sub in enumerate(subs):
+                if k == 0 and a == 0 and b == 0:
+                    coeff_in[phase, me] = coeff_out[phase, me]
+                    continue
+                remote(
+                    coeff_out.at[phase, col * sub_count + sub], coeff_in.at[phase, me], phase,
+                    col, sub, arrival_of(phase, my_group),
+                ).start()
 
     def all_of(blocks, slot):
         return remote(blocks, blocks, slot, my_col, subs[1])
@@ -145,23 +163,34 @@
         gram_in[which, me] = gram_out[which]
 
     def far_field(phase):
-        for m in range(tiles // 2):
-            even, odd = coeff_in[phase, 2 * m], coeff_in[phase, 2 * m + 1]
-            upper = jnp.where(in_first, even, swap(odd))
-            lower = jnp.where(in_first, swap(even), odd)
-            gathered[:, m * 128:(m + 1) * 128] = split_rows(jnp.concatenate([upper, lower], axis=0))
-        return join_rows(dot_rows(gathered[...], left[...]))
+        total = 0.0
+        for k in range(chunks):
+            blocks = coeff_in.at[phase, pl.ds(0, group_tiles - (k == 0))]
+            remote(
+                blocks, blocks, phase, my_col, subs[1], arrival_of(phase, groups[k])
+            ).wait_recv()
+            pairs = []
+            for m in range(group_tiles // 2):
+                at = groups[k] * group_tiles + 2 * m
+                even, odd = coeff_in[phase, at], coeff_in[phase, at + 1]
+                upper = jnp.where(in_first, even, swap(odd))
+                lower = jnp.where(in_first, swap(even), odd)
+                pairs.append(split_rows(jnp.concatenate([upper, lower], axis=0)))
+            total = total + join_rows(dot_rows(jnp.concatenate(pairs, axis=1), left[:, span(k)]))
+        return total
 
     rhs = rhs_ref[...]
     diag = diag_ref[...]
     stacked = split_rows(rhs)
-    project(stacked, 0, True)
+    for load, k in zip(right_loads, outward):
+        load.wait()
+        project(stacked, 0, k)
     pl.semaphore_wait(barrier, tiles - 1)
-    send_coefficients(0)
+    for k in outward:
+        send_group(0, k)
     near_load.wait()
     moved = (diag - SHIFT) * rhs + join_rows(dot_rows(stacked, near[...]))
     left_load.wait()
-    coefficients_of(0).wait_recv()
     moved = moved + far_field(0)
     image_1 = moved + SHIFT * rhs
 
@@ -174,12 +203,12 @@
     )
     first_store.start()
     stacked = split_rows(moved)
-    project(stacked, 1, False)
-    send_coefficients(1)
+    for k in outward:
+        project(stacked, 1, k)
+        send_group(1, k)
     early = dot_rows(image_1, jnp.concatenate([rhs, image_1], axis=0), highest)
     send_gram(0, jnp.concatenate([early, jnp.zeros_like(early)], axis=1))
     image_2 = diag * moved + join_rows(dot_rows(stacked, near[...]))
-    coefficients_of(1).wait_recv()
     image_2 = image_2 + far_field(1)
 
     vectors[2 * count:] = image_2
@@ -247,7 +276,7 @@
     rhs_count, cells = right_sides.shape
     tiles, rank_len, _ = right_bases.shape
     features = tiles * rank_len
-    chunk = min(512, features)
+    chunk = max(features // 4, rank_len * sub_count)
     vmem = pl.BlockSpec(memory_space=pltpu.VMEM)
     anywhere = pl.BlockSpec(memory_space=pl.ANY)
     vectors, system = pl.pallas_call(
@@ -272,10 +301,10 @@
             pltpu.VMEM((2, tiles, 8, 128), jnp.float32),
             pltpu.VMEM((2, 8, 128), jnp.float32),
             pltpu.VMEM((2, tiles, 8, 128), jnp.float32),
-            pltpu.VMEM((2 * rhs_count, features), jnp.bfloat16),
+            pltpu.VMEM((tiles // 2, 128), jnp.float32),
             pltpu.SemaphoreType.DMA((features // chunk + 9,)),
             pltpu.SemaphoreType.DMA((4,)),
-            pltpu.SemaphoreType.DMA((4,)),
+            pltpu.SemaphoreType.DMA((4 + 2 * (features // chunk),)),
         ],
         compiler_params=pltpu.CompilerParams(
             collective_id=0, has_side_effects=True, vmem_limit_bytes=VMEM_BYTES

time: 30.9 us -> 30 us (0.971)
  Pallas kernels: 30.1 us -> 29.2 us
    pallas_call x1, Pallas kernels: 28.3 us -> 27.4 us  [on_device(): pl.pallas_call(functools.partial(kernel, col_count, sub_count, tiles, chu...]
where the time goes in v4:
time: 30 us; the launch traced here: 29.8 us
  Pallas kernels  29.2 us (97%)
  between operations  0.64 us (2%)
    pallas_call x1, Pallas kernels, on_device(): pl.pallas_call(functools.partial(kernel, col_count, sub_count, tiles, chu...  27.4 us
    pallas_call x1, Pallas kernels, on_device(): pl.pallas_call(combine, out_shape=[jax.ShapeDtypeStruct((rhs_count, cells...  1.78 us

profile of v4, /device:TPU:0, one launch (start us, length us, event | category | flops | bytes accessed | tf_op | source)
XLA Modules:
  0.0 29.8 jit_solution(8747903613101742810)
XLA Ops:
  0.6 27.4 %shard_map.86 = (f32[48,512]{1,0:T(8,128)}, f32[32,128]{1,0:T(8,128)}) custom-call(f32[16,512]{1,0:T(8,128)} %rhs_ref.1, f32[32,64]{1,0:T(8,128)} %bitcast.5, s32[1,32]{1,0:T(1,128)} %bitcast.7, f32[1,512]{1,0:T(1,128)} %bitcast.6, bf16[2048,512]{1,0:T(8,128)(2,1)} %bitcast.4, bf16[512,2048]{1,0:T(8,128)(2,1)} %left_hbm.1, bf16[512,512]{1,0:T(8,128)(2,1)} %near_hbm.1), custom_call_target="tpu_custom_call" | custom-call | tf_op jit(solution)/shard_map/pallas_call | solution.py:282
  28.1 1.8 %shard_map.87 = (f32[16,512]{1,0:T(8,128)}, f32[16,512]{1,0:T(8,128)}) custom-call(f32[16,512]{1,0:T(8,128)} %rhs_ref.1, f32[48,512]{1,0:T(8,128)} %get-tuple-element.4.vectors_ref, f32[32,128]{1,0:T(8,128)} %get-tuple-element.5.system_ref), custom_call_target="tpu_custom_call" | custom-call | tf_op jit(solution)/shard_map/pallas_call | solution.py:321

commit v5 on v4

--- a/solution.py
+++ b/solution.py
@@ -184,10 +184,12 @@
     stacked = split_rows(rhs)
     for load, k in zip(right_loads, outward):
         load.wait()
+        if k == 0:
+            pl.semaphore_wait(barrier, tiles - 1)
+            for sent in outward[:-1]:
+                send_group(0, sent)
         project(stacked, 0, k)
-    pl.semaphore_wait(barrier, tiles - 1)
-    for k in outward:
-        send_group(0, k)
+    send_group(0, 0)
     near_load.wait()
     moved = (diag - SHIFT) * rhs + join_rows(dot_rows(stacked, near[...]))
     left_load.wait()

time: 30 us -> 29.7 us (0.990)
  Pallas kernels: 29.2 us -> 28.9 us
    pallas_call x1, Pallas kernels: 27.4 us -> 27.1 us  [on_device(): pl.pallas_call(functools.partial(kernel, col_count, sub_count, tiles, chu...]
where the time goes in v5:
time: 29.7 us; the launch traced here: 29.5 us
  Pallas kernels  28.9 us (97%)
  between operations  0.64 us (2%)
    pallas_call x1, Pallas kernels, on_device(): pl.pallas_call(functools.partial(kernel, col_count, sub_count, tiles, chu...  27.1 us
    pallas_call x1, Pallas kernels, on_device(): pl.pallas_call(combine, out_shape=[jax.ShapeDtypeStruct((rhs_count, cells...  1.79 us

profile of v5, /device:TPU:0, one launch (start us, length us, event | category | flops | bytes accessed | tf_op | source)
XLA Modules:
  0.0 29.5 jit_solution(13986366985375299983)
XLA Ops:
  0.6 27.1 %shard_map.86 = (f32[48,512]{1,0:T(8,128)}, f32[32,128]{1,0:T(8,128)}) custom-call(f32[16,512]{1,0:T(8,128)} %rhs_ref.1, f32[32,64]{1,0:T(8,128)} %bitcast.5, s32[1,32]{1,0:T(1,128)} %bitcast.7, f32[1,512]{1,0:T(1,128)} %bitcast.6, bf16[2048,512]{1,0:T(8,128)(2,1)} %bitcast.4, bf16[512,2048]{1,0:T(8,128)(2,1)} %left_hbm.1, bf16[512,512]{1,0:T(8,128)(2,1)} %near_hbm.1), custom_call_target="tpu_custom_call" | custom-call | tf_op jit(solution)/shard_map/pallas_call | solution.py:284
  27.7 1.8 %shard_map.87 = (f32[16,512]{1,0:T(8,128)}, f32[16,512]{1,0:T(8,128)}) custom-call(f32[16,512]{1,0:T(8,128)} %rhs_ref.1, f32[48,512]{1,0:T(8,128)} %get-tuple-element.4.vectors_ref, f32[32,128]{1,0:T(8,128)} %get-tuple-element.5.system_ref), custom_call_target="tpu_custom_call" | custom-call | tf_op jit(solution)/shard_map/pallas_call | solution.py:323
